TPU v7x, 256 devices: a whole 4x4x8 slice. The times are simulated.
256 devices in a mesh: lat: 16 (over z_lo, y, core), lev: 4 (over x), ocn: 4 (over z_hi).
Axes of the slice: x: 4, y: 4, z: 8 (z_hi: 4, z_lo: 2; z = z_hi * 2 + z_lo), core: 2. Of those that a mesh axis runs over, the one named last changes fastest.
Arguments:
- atmos_fields: bfloat16 [2, 24, 2560, 5632], P(None, 'lev', ('lat', 'ocn')), may hold values from -6 to 6
- lat_points: int32 [2560], P(('lat', 'ocn')), may hold values from 20 to 5632, as said below
- wave_order: int32 [256], replicated, may hold values from 0 to 255, each once
- legendre: bfloat16 [256, 2560, 1536], P(('lat', 'ocn'), None, 'lev'), may hold values from -0.125 to 0.125
- column_weight: bfloat16 [2, 24], P(None, 'lev'), may hold values from -1.25 to 1.25
- block_remap: int32 [2560, 44], P(('lat', 'ocn'), 'lev'), may hold values from 0 to 17407, as said below
- ocean_temp: float32 [1024, 2176], P(('lat', 'ocn')), may hold values from -6 to 6
- ocean_salt: float32 [1024, 2176], P(('lat', 'ocn')), may hold values from -6 to 6
- sea_mask: int32 [1024, 17], P(('lat', 'ocn')), may hold values 0 or 1
Outputs:
- spectra: float32 [256, 96, 1536], P(('lat', 'ocn'), None, 'lev')
- temp_next: float32 [1024, 2176], P(('lat', 'ocn'))
- salt_next: float32 [1024, 2176], P(('lat', 'ocn'))
- surface_temp: float32 [2560, 5632], P(('lat', 'ocn'), 'lev')
Inputs may be any that keep to these rules, and one draw needn't show every extreme that they name: `lat_points`: a multiple of 4 for every latitude row. `wave_order`: each wavenumber appears once. `block_remap`: the blocks of latitude band g (rows g * 40 onward) name tiles of ocean sections g - 1, g or g + 1 only; section g holds tiles g * 16 * 17 onward, in row order.
All inputs are finite; a program needn't handle non-finite values. No bound on the sum of `sea_mask` on one device may be relied on, other than what follows from the above.
Results may differ from a plain program's by a relative error of at most 0.0037.
Values may be sent and summed in bfloat16 or wider, within the bound.
A program may use at most 128 MiB of HBM per device.

v0:
```python
import math
import jax
import jax.numpy as jnp
from jax import lax
from jax.sharding import PartitionSpec as P

FIELDS = 2
BLOCK = 128
FULL_TURN = 2.0 * math.pi
DIFFUSION = 0.2
COUPLING = 0.5


def with_halo(cells, sides, width):
    for axis, dim in sides:
        count = lax.axis_size(axis)
        ends = count - 1
        head = lax.slice_in_dim(cells, 0, width, axis=dim)
        tail = lax.slice_in_dim(cells, cells.shape[dim] - width, cells.shape[dim], axis=dim)
        cells = jnp.concatenate(
            [
                lax.ppermute(tail, axis, [(i, (i + 1) % count) for i in range(ends)]),
                cells,
                lax.ppermute(head, axis, [((i + 1) % count, i) for i in range(ends)]),
            ],
            axis=dim,
        )
    return cells


def fourier_table(wave_order, length):
    points = jnp.arange(length, dtype=jnp.int32)
    phase = wave_order[None, :] * points[:, None] % length
    angle = phase.astype(jnp.float32) * (FULL_TURN / length)
    table = jnp.concatenate([jnp.cos(angle), -jnp.sin(angle)], axis=1).astype(jnp.bfloat16)
    return (table, points)


def body(
    atmos_fields,
    lat_points,
    wave_order,
    legendre,
    column_weight,
    block_remap,
    ocean_temp,
    ocean_salt,
    sea_mask,
):
    nfields, lev_dev, lat_band, lon_count = atmos_fields.shape
    wave_count = wave_order.shape[0]
    table, points = fourier_table(wave_order, lon_count)
    point_mask = points[None, :] < lat_points[:, None]
    masked = jnp.where(point_mask[None, None], atmos_fields, jnp.zeros((), jnp.bfloat16))
    inverse_root = 1.0 / jnp.sqrt(lat_points.astype(jnp.float32))
    weights = jnp.where(
        2 * wave_order[None, :] < lat_points[:, None],
        inverse_root[:, None],
        jnp.zeros((), jnp.float32),
    )
    field_count = masked.shape[0]
    raw_sums = jnp.dot(masked.reshape(-1, lon_count), table, preferred_element_type=jnp.float32)
    raw_sums = raw_sums.reshape(field_count, lev_dev, lat_band, 2, wave_count)
    coeffs = (raw_sums * weights[None, None, :, None, :]).astype(jnp.bfloat16)
    regrouped = lax.all_to_all(
        coeffs.transpose(4, 1, 0, 3, 2).reshape(wave_count, lev_dev * field_count * 2, lat_band),
        ("lat", "ocn"),
        split_axis=0,
        concat_axis=2,
        tiled=True,
    )
    spectra = jnp.einsum(
        "srj,sjd->srd",
        lax.all_gather(regrouped, "lev", axis=1, tiled=True),
        legendre,
        preferred_element_type=jnp.float32,
    )
    ocean_rows, ocean_cols = ocean_temp.shape
    tile_count = ocean_rows * ocean_cols // BLOCK
    band_index = lax.axis_index(("lat", "ocn"))
    targets = block_remap.reshape(-1)
    local_slot = (targets // tile_count - band_index + 1) * tile_count + targets % tile_count
    partial_sum = jnp.einsum(
        "ql,qljk->qjk", column_weight, masked, preferred_element_type=jnp.float32
    )
    quarter = lon_count // lax.axis_size("lev")
    totals = lax.psum(partial_sum, "lev")
    own_flux = lax.dynamic_slice_in_dim(totals, lax.axis_index("lev") * quarter, quarter, 2)
    block_rows = (
        own_flux.reshape(FIELDS, lat_band, quarter // BLOCK, BLOCK)
        .transpose(1, 2, 0, 3)
        .reshape(-1, FIELDS * BLOCK)
    )
    outgoing = jax.ops.segment_sum(block_rows, local_slot, num_segments=3 * tile_count)
    widened = with_halo(outgoing, ((("lat", "ocn"), 0),), tile_count)
    arrived = (
        widened[:tile_count] + widened[2 * tile_count : 3 * tile_count] + widened[4 * tile_count :]
    )
    tile_sums = lax.psum(arrived, "lev")
    forcing = (
        tile_sums.reshape(ocean_rows, ocean_cols // BLOCK, FIELDS, BLOCK)
        .transpose(2, 0, 1, 3)
        .reshape(FIELDS, ocean_rows, ocean_cols)
    )
    sea_cells = (
        jnp.broadcast_to(sea_mask[:, :, None], (ocean_rows, ocean_cols // BLOCK, BLOCK))
        .reshape(ocean_rows, ocean_cols)
        .astype(jnp.float32)
    )
    ocean_state = jnp.stack([ocean_temp, ocean_salt])
    padded = with_halo(ocean_state, ((("lat", "ocn"), 1),), 1)
    laplace = (
        padded[:, 2:]
        + padded[:, :-2]
        + jnp.roll(ocean_state, 1, 2)
        + jnp.roll(ocean_state, -1, 2)
        - 4.0 * ocean_state
    )
    updated = ocean_state + DIFFUSION * laplace + COUPLING * sea_cells[None] * forcing
    temp_next = updated[0]
    salt_next = updated[1]
    returned = with_halo(temp_next, ((("lat", "ocn"), 0),), ocean_rows)
    tiles_near = returned.reshape(3 * tile_count, BLOCK)
    surface = jnp.take(tiles_near, local_slot, axis=0).reshape(lat_band, quarter)
    own_points = lax.axis_index("lev") * quarter + jnp.arange(quarter, dtype=jnp.int32)
    surface_temp = jnp.where(
        own_points[None, :] < lat_points[:, None], surface, jnp.zeros((), jnp.float32)
    )
    return (spectra, temp_next, salt_next, surface_temp)


def solution(mesh):
    placed = (
        P(None, "lev", ("lat", "ocn"), None),
        P(("lat", "ocn")),
        P(),
        P(("lat", "ocn"), None, "lev"),
        P(None, "lev"),
        P(("lat", "ocn"), "lev"),
        P(("lat", "ocn"), None),
        P(("lat", "ocn"), None),
        P(("lat", "ocn"), None),
    )
    return jax.shard_map(
        body,
        mesh=mesh,
        in_specs=placed,
        out_specs=(
            P(("lat", "ocn"), None, "lev"),
            P(("lat", "ocn"), None),
            P(("lat", "ocn"), None),
            P(("lat", "ocn"), "lev"),
        ),
        check_vma=False,
    )
```

profile of v0, /device:TPU:1, one launch (start us, length us, event | category | flops | bytes accessed | tf_op | source)
XLA Modules:
  0.0 199.3 jit_solution(3094316823144433169)
XLA Ops:
  7.2 0.8 iota_compare_fusion
  8.1 3.6 %broadcast_select_fusion = bf16[2,6,40,5632]{3,2,1,0:T(8,128)(2,1)S(1)} fusion(bf16[2,6,40,5632]{3,2,1,0:T(8,128)(2,1)} %param.9, pred[40,5632]{1,0:T(8,128)(4,1)S(1)} %iota_compare_fusion), kind=kLoop, calls=%fused_computation.16 | loop fusion | flops 2703360 | bytes 11038720 | tf_op jit(solution)/shard_map/jit(_where)/select_n | solution.py:54
  11.7 2.4 %fusion = f32[2,1,40,5632]{3,1,2,0:T(1,128)S(1)} fusion(bf16[2,6,40,5632]{3,2,1,0:T(8,128)(2,1)S(1)} %broadcast_select_fusion, bf16[2,6,1,1]{1,0,2,3:T(2,128)(2,1)S(1)} %bitcast.59), kind=kOutput, calls=%fused_computation.3 | convolution fusion | flops 5406720 | bytes 7208984 | tf_op jit(solution)/shard_map/ql,qljk->qjk/dot_general | solution.py:83
  14.2 1.4 copy.59
  15.6 25.0 %cosine_convert_fusion = (bf16[5632,256]{0,1:T(8,128)(2,1)S(1)}, bf16[5632,256]{0,1:T(8,128)(2,1)S(1)}) fusion(s32[256]{0:T(256)S(1)} %copy-done.8), kind=kLoop, calls=%fused_computation.9 | loop fusion | flops 17301504 | bytes 5768192 | tf_op jit(solution)/shard_map/convert
  40.7 2.9 %pad_maximum_fusion = bf16[5632,512]{0,1:T(8,128)(2,1)} fusion(bf16[5632,256]{0,1:T(8,128)(2,1)S(1)} %get-tuple-element.21, bf16[5632,256]{0,1:T(8,128)(2,1)S(1)} %get-tuple-element.20), kind=kLoop, calls=%fused_computation.7 | loop fusion | flops 11534336 | bytes 11534336 | tf_op jit(solution)/shard_map/concatenate | solution.py:35
  43.6 5.7 %fusion.15 = bf16[256,6,2,2,40]{0,4,3,1,2:T(8,128)(2,1)S(1)} fusion(bf16[2,256,5632,1,1]{2,1,0,4,3:T(8,128)(2,1)} %bitcast.64, bf16[2,6,40,5632]{3,2,1,0:T(8,128)(2,1)S(1)} %bitcast.61, f32[256,40]{0,1:T(8,128)S(1)} %compare_select_fusion), kind=kOutput, calls=%fused_computation.20 | convolution fusion | flops 2768732160 | bytes 11706368 | tf_op jit(solution)/shard_map/dot_general | solution.py:62
  49.4 1.0 copy.32
  50.3 3.4 %reshape.235 = bf16[64,2,1920]{2,1,0:T(2,128)(2,1)} reshape(bf16[256,24,40]{2,1,0:T(8,128)(2,1)S(1)} %copy.32) | data formatting | bytes 983040
  53.7 13.3 %all-to-all-start = ((bf16[64,2,1920]{2,1,0:T(2,128)(2,1)}), bf16[64,2,1920]{2,1,0:T(2,128)(2,1)S(1)}, u32[]{:S(2)}, u32[]{:S(2)}) async-start(bf16[64,2,1920]{2,1,0:T(2,128)(2,1)} %reshape.235), calls=%async_computation | async-start | bytes 983040 | tf_op jit(solution)/shard_map/all_to_all | solution.py:65
  67.2 0.1 copy.35
  67.2 0.1 rem.47
  67.4 0.1 copy.36
  67.5 0.1 div.26
  67.6 0.1 copy.34
  67.7 0.1 ne.88
  67.9 10.6 %all-reduce.3.cloned.1.call-done = f32[2,40,5632]{2,1,0:T(8,128)} async-done(((f32[2,40,5632]{2,1,0:T(8,128)}), f32[2,40,5632]{2,1,0:T(8,128)}) %all-reduce.3.cloned.1.call-update) | async-done | bytes 1802256 | tf_op jit(solution)/shard_map/psum | solution.py:87
  78.5 1.0 constant_dynamic-slice_fusion
  79.6 0.1 reshape.208
  79.6 0.3 copy.37
  80.0 3.1 %scatter_custom_fusion = f32[816,256]{1,0:T(8,128)S(1)} fusion(s32[440]{0:T(512)S(1)} %bitcast.81, f32[55,8,2,128]{3,2,1,0:T(2,128)S(1)} %bitcast.75, f32[]{:T(128)} %constant.40.clone.1), kind=kCustom, calls=%fused_computation.35 | custom fusion | flops 112640 | bytes 1286148 | tf_op jit(solution)/shard_map/scatter-add | solution.py:94
  83.2 6.3 %collective-permute-start.3 = (f32[272,256]{1,0:T(8,128)S(1)}, f32[272,256]{1,0:T(8,128)S(1)}, u32[]{:S(2)}, u32[]{:S(2)}) collective-permute-start(f32[272,256]{1,0:T(8,128)S(1)} %get-tuple-element.9), channel_id=1, source_target_pairs={{1,0},{2,1},{3,2},{16,3},{17,16},{18,17},{19,18},{32,19},{33,32},{... | collective-permute-start | bytes 835592 | tf_op jit(solution)/shard_map/ppermute | solution.py:24
  89.5 1.9 collective-permute-start.2
  91.4 8.1 %collective-permute-done.3 = f32[272,256]{1,0:T(8,128)S(1)} collective-permute-done((f32[272,256]{1,0:T(8,128)S(1)}, f32[272,256]{1,0:T(8,128)S(1)}, u32[]{:S(2)}, u32[]{:S(2)}) %collective-permute-start.3) | collective-permute-done | bytes 278560 | tf_op jit(solution)/shard_map/ppermute | solution.py:24
  99.6 8.0 %collective-permute-done.2 = f32[272,256]{1,0:T(8,128)S(1)} collective-permute-done((f32[272,256]{1,0:T(8,128)S(1)}, f32[272,256]{1,0:T(8,128)S(1)}, u32[]{:S(2)}, u32[]{:S(2)}) %collective-permute-start.2) | collective-permute-done | bytes 278560 | tf_op jit(solution)/shard_map/ppermute | solution.py:22
  107.7 0.1 reshape.210
  107.9 0.8 reshape.211
  108.7 1.9 collective-permute-start.1
  110.7 5.8 %collective-permute-start = (f32[2,1,2176]{2,1,0:T(1,128)S(1)}, f32[2,1,2176]{2,1,0:T(1,128)S(1)}, u32[]{:S(2)}, u32[]{:S(2)}) collective-permute-start(f32[2,1,2176]{2,1,0:T(1,128)S(1)} %get-tuple-element.16), channel_id=1, source_target_pairs={{1,0},{2,1},{3,2},{16,3},{17,16},{18,17},{19,18},{32,19},{33,32},{... | collective-permute-start | bytes 52232 | tf_op jit(solution)/shard_map/ppermute | solution.py:24
  116.4 2.5 %reshape.236 = bf16[256,24,40]{2,1,0:T(8,128)(2,1)S(1)} reshape(bf16[64,2,1920]{2,1,0:T(2,128)(2,1)S(1)} %all-to-all-done) | data formatting | bytes 983040
  119.0 0.6 copy.33
  119.6 3.9 %all_to_all.16 = bf16[4,24,2560]{2,1,0:T(8,128)(2,1)} reshape(bf16[4,24,64,40]{3,2,1,0:T(8,128)(2,1)S(1)} %copy.33) | data formatting | bytes 983040 | tf_op jit(solution)/shard_map/all_to_all | solution.py:65
  123.5 0.1 fusion.23
  123.6 0.1 fusion.35
  123.7 0.1 broadcast_in_dim.66
  123.9 25.7 %all-reduce.5.cloned.1.call-done = f32[2,16,2176]{2,1,0:T(8,128)} async-done(((f32[2,16,2176]{2,1,0:T(8,128)}), f32[2,16,2176]{2,1,0:T(8,128)}) %all-reduce.5.cloned.1.call-update) | async-done | bytes 278544 | tf_op jit(solution)/shard_map/psum | solution.py:99
  149.5 1.2 fusion.31
  150.7 0.7 slice_bitcast_fusion
  151.4 8.4 %collective-permute-start.5 = (f32[16,2176]{1,0:T(8,128)S(1)}, f32[16,2176]{1,0:T(8,128)S(1)}, u32[]{:S(2)}, u32[]{:S(2)}) collective-permute-start(f32[16,2176]{1,0:T(8,128)S(1)} %get-tuple-element.11), channel_id=1, source_target_pairs={{1,0},{2,1},{3,2},{16,3},{17,16},{18,17},{19,18},{32,19},{33,32},{... | collective-permute-start | bytes 417800 | tf_op jit(solution)/shard_map/ppermute | solution.py:24
  159.8 1.9 collective-permute-start.4
  161.7 0.1 copy.39
  161.9 2.9 %collective-permute-done.5 = f32[16,2176]{1,0:T(8,128)S(1)} collective-permute-done((f32[16,2176]{1,0:T(8,128)S(1)}, f32[16,2176]{1,0:T(8,128)S(1)}, u32[]{:S(2)}, u32[]{:S(2)}) %collective-permute-start.5) | collective-permute-done | bytes 139296 | tf_op jit(solution)/shard_map/ppermute | solution.py:24
  164.8 5.0 %collective-permute-done.4 = f32[16,2176]{1,0:T(8,128)S(1)} collective-permute-done((f32[16,2176]{1,0:T(8,128)S(1)}, f32[16,2176]{1,0:T(8,128)S(1)}, u32[]{:S(2)}, u32[]{:S(2)}) %collective-permute-start.4) | collective-permute-done | bytes 139296 | tf_op jit(solution)/shard_map/ppermute | solution.py:22
  169.8 1.2 gather_fusion
  171.1 0.1 broadcast_in_dim.68
  171.2 0.8 select_select_fusion
  172.0 14.7 %all-gather.2.cloned.1.call-done = bf16[4,96,2560]{2,1,0:T(8,128)(2,1)} async-done(((bf16[4,24,2560]{2,1,0:T(8,128)(2,1)}), bf16[4,96,2560]{2,1,0:T(8,128)(2,1)}) %all-gather.2.cloned.1.call-update) | async-done | bytes 1966096 | tf_op jit(solution)/shard_map/all_gather | solution.py:74
  186.7 6.1 %fusion.44 = f32[4,96,384]{2,1,0:T(8,128)} fusion(bf16[4,96,2560]{2,1,0:T(8,128)(2,1)} %all-gather.2.cloned.1.call-done, bf16[4,2560,384]{2,1,0:T(8,128)(2,1)} %param.12), kind=kOutput, calls=%fused_computation.87 | convolution fusion | flops 754974720 | bytes 10420224 | tf_op jit(solution)/shard_map/srj,sjd->srd/dot_general | solution.py:72
  (50 shorter events, 0.7 us)
Async XLA Ops:
  7.2 4.5 %copy-start = (bf16[2,6]{1,0:T(2,128)(2,1)S(1)}, bf16[2,6]{1,0:T(2,128)(2,1)}, u32[]{:S(2)}) copy-start(bf16[2,6]{1,0:T(2,128)(2,1)} %param.13) | copy-start | bytes 76
  7.2 71.3 %all-reduce.3.cloned.1.call-start = ((), (), s32[]{:S(2)}) async-start(), calls=%async_computation.2 | async-start | bytes 3604480 | tf_op jit(solution)/shard_map/psum | solution.py:87
  11.7 3.8 %copy-start.1 = (bf16[2,6,40,5632]{3,2,1,0:T(8,128)(2,1)}, bf16[2,6,40,5632]{3,2,1,0:T(8,128)(2,1)S(1)}, u32[]{:S(2)}) copy-start(bf16[2,6,40,5632]{3,2,1,0:T(8,128)(2,1)S(1)} %broadcast_select_fusion) | copy-start | bytes 16220164
  11.7 3.8 %copy-start.7 = (s32[40]{0:T(128)S(1)}, s32[40]{0:T(128)}, u32[]{:S(2)}) copy-start(s32[40]{0:T(128)} %param.10) | copy-start | bytes 484
  11.7 3.8 %copy-start.8 = (s32[256]{0:T(256)S(1)}, s32[256]{0:T(256)}, u32[]{:S(2)}) copy-start(s32[256]{0:T(256)} %param.11) | copy-start | bytes 3076
  15.6 28.0 %slice-start = ((s8[5406720]{0:T(1024)(128)(4,1)}), s8[4194304]{0:T(1024)(128)(4,1)S(1)}, s32[]{:S(2)}) async-start(s8[5406720]{0:T(1024)(128)(4,1)} %bitcast.60), calls=%async_computation.4 | async-start | bytes 8388608
  40.6 3.0 %slice-start.1 = ((s8[5406720]{0:T(1024)(128)(4,1)}), s8[1212416]{0:T(1024)(128)(4,1)S(1)}, s32[]{:S(2)}) async-start(s8[5406720]{0:T(1024)(128)(4,1)} %bitcast.60), calls=%async_computation.5 | async-start | bytes 2424832
  49.3 17.8 %copy-start.5 = (s32[40,11]{0,1:T(8,128)S(1)}, s32[40,11]{0,1:T(8,128)}, u32[]{:S(2)}) copy-start(s32[40,11]{0,1:T(8,128)} %param.14) | copy-start | bytes 5284
  53.7 54.9 %copy-start.2 = (f32[16,2176]{1,0:T(8,128)S(1)}, f32[16,2176]{1,0:T(8,128)}, u32[]{:S(2)}) copy-start(f32[16,2176]{1,0:T(8,128)} %param.15) | copy-start | bytes 417796
  53.7 54.9 %copy-start.3 = (f32[16,2176]{1,0:T(8,128)S(1)}, f32[16,2176]{1,0:T(8,128)}, u32[]{:S(2)}) copy-start(f32[16,2176]{1,0:T(8,128)} %param.16) | copy-start | bytes 417796
  53.7 62.7 %all-to-all-start = ((bf16[64,2,1920]{2,1,0:T(2,128)(2,1)}), bf16[64,2,1920]{2,1,0:T(2,128)(2,1)S(1)}, u32[]{:S(2)}, u32[]{:S(2)}) async-start(bf16[64,2,1920]{2,1,0:T(2,128)(2,1)} %reshape.235), calls=%async_computation | async-start | bytes 983040 | tf_op jit(solution)/shard_map/all_to_all | solution.py:65
  67.1 82.5 %all-reduce.5.cloned.1.call-start = ((), (), s32[]{:S(2)}) async-start(), calls=%async_computation.3 | async-start | bytes 557056 | tf_op jit(solution)/shard_map/psum | solution.py:99
  83.2 16.4 %collective-permute-start.3 = (f32[272,256]{1,0:T(8,128)S(1)}, f32[272,256]{1,0:T(8,128)S(1)}, u32[]{:S(2)}, u32[]{:S(2)}) collective-permute-start(f32[272,256]{1,0:T(8,128)S(1)} %get-tuple-element.9), channel_id=1, source_target_pairs={{1,0},{2,1},{3,2},{16,3},{17,16},{18,17},{19,18},{32,19},{33,32},{... | collective-permute-start | bytes 835592 | tf_op jit(solution)/shard_map/ppermute | solution.py:24
  89.5 18.1 %collective-permute-start.2 = (f32[272,256]{1,0:T(8,128)S(1)}, f32[272,256]{1,0:T(8,128)S(1)}, u32[]{:S(2)}, u32[]{:S(2)}) collective-permute-start(f32[272,256]{1,0:T(8,128)S(1)} %get-tuple-element.8), channel_id=1, source_target_pairs={{0,1},{1,2},{2,3},{3,16},{16,17},{17,18},{18,19},{19,32},{32,33},{... | collective-permute-start | bytes 835592 | tf_op jit(solution)/shard_map/ppermute | solution.py:22
  107.6 15.8 %copy-start.6 = (s32[16,17]{1,0:T(8,128)S(1)}, s32[16,17]{1,0:T(8,128)}, u32[]{:S(2)}) copy-start(s32[16,17]{1,0:T(8,128)} %param.17) | copy-start | bytes 3268
  108.6 78.1 %all-gather.2.cloned.1.call-start = ((), (), s32[]{:S(2)}) async-start(), calls=%async_computation.1 | async-start | bytes 2457600 | tf_op jit(solution)/shard_map/all_gather | solution.py:74
  108.7 15.1 %collective-permute-start.1 = (f32[2,1,2176]{2,1,0:T(1,128)S(1)}, f32[2,1,2176]{2,1,0:T(1,128)S(1)}, u32[]{:S(2)}, u32[]{:S(2)}) collective-permute-start(f32[2,1,2176]{2,1,0:T(1,128)S(1)} %get-tuple-element.17), channel_id=1, source_target_pairs={{0,1},{1,2},{2,3},{3,16},{16,17},{17,18},{18,19},{19,32},{32,33},{... | collective-permute-start | bytes 52232 | tf_op jit(solution)/shard_map/ppermute | solution.py:22
  110.7 13.2 %collective-permute-start = (f32[2,1,2176]{2,1,0:T(1,128)S(1)}, f32[2,1,2176]{2,1,0:T(1,128)S(1)}, u32[]{:S(2)}, u32[]{:S(2)}) collective-permute-start(f32[2,1,2176]{2,1,0:T(1,128)S(1)} %get-tuple-element.16), channel_id=1, source_target_pairs={{1,0},{2,1},{3,2},{16,3},{17,16},{18,17},{19,18},{32,19},{33,32},{... | collective-permute-start | bytes 52232 | tf_op jit(solution)/shard_map/ppermute | solution.py:24
  151.4 41.4 %copy-start.4 = (f32[16,2176]{1,0:T(8,128)}, f32[16,2176]{1,0:T(8,128)S(1)}, u32[]{:S(2)}) copy-start(f32[16,2176]{1,0:T(8,128)S(1)} %get-tuple-element.11) | copy-start | bytes 417796
  151.4 13.4 %collective-permute-start.5 = (f32[16,2176]{1,0:T(8,128)S(1)}, f32[16,2176]{1,0:T(8,128)S(1)}, u32[]{:S(2)}, u32[]{:S(2)}) collective-permute-start(f32[16,2176]{1,0:T(8,128)S(1)} %get-tuple-element.11), channel_id=1, source_target_pairs={{1,0},{2,1},{3,2},{16,3},{17,16},{18,17},{19,18},{32,19},{33,32},{... | collective-permute-start | bytes 417800 | tf_op jit(solution)/shard_map/ppermute | solution.py:24
  159.8 10.0 %collective-permute-start.4 = (f32[16,2176]{1,0:T(8,128)S(1)}, f32[16,2176]{1,0:T(8,128)S(1)}, u32[]{:S(2)}, u32[]{:S(2)}) collective-permute-start(f32[16,2176]{1,0:T(8,128)S(1)} %get-tuple-element.11), channel_id=1, source_target_pairs={{0,1},{1,2},{2,3},{3,16},{16,17},{17,18},{18,19},{19,32},{32,33},{... | collective-permute-start | bytes 417800 | tf_op jit(solution)/shard_map/ppermute | solution.py:22
Sparse Core Ops, SparseCore 0:
  15.7 62.7 all-reduce.2
  108.7 40.7 all-reduce.4
  152.1 34.6 all-gather.1
where the time goes:
time: 200 us; the launch traced here: 199 us
  waiting for transfers between devices  75.1 us (38%)
  starting transfers between devices  39.7 us (20%)
  other arithmetic  37.9 us (19%)
  local copies, waits for them, and re-layouts  18.2 us (9%)
  matrix products  14.2 us (7%)
  between operations  14.2 us (7%)
    psum x1, waiting for transfers between devices, body(): tile_sums = lax.psum(arrived, 'lev')  25.7 us
    another operation x1, other arithmetic  25 us
    ppermute x3, starting transfers between devices, with_halo(): lax.ppermute(head, axis, [((i + 1) % count, i) for i in range(ends)])  20.5 us
    all_gather x1, waiting for transfers between devices, body(): lax.all_gather(regrouped, 'lev', axis=1, tiled=True)  14.7 us
    all_to_all x1, starting transfers between devices, body(): lax.all_to_all(coeffs.transpose(4, 1, 0, 3, 2).reshape(wave_count, lev_de...  13.3 us
    ppermute x3, waiting for transfers between devices, with_halo(): lax.ppermute(tail, axis, [(i, (i + 1) % count) for i in range(ends)])  13 us
    ppermute x3, waiting for transfers between devices, with_halo(): lax.ppermute(head, axis, [((i + 1) % count, i) for i in range(ends)])  11.1 us
    psum x1, waiting for transfers between devices, body(): totals = lax.psum(partial_sum, 'lev')  10.6 us
  transfers between devices with their start and end apart: 10, of which 7 were waited for; matrix products, arithmetic and copies ran while one was open for 26% of the time, Pallas kernels for 0%

commit v1 on v0

--- a/solution.py
+++ b/solution.py
@@ -47,6 +47,17 @@
     ocean_salt,
     sea_mask,
 ):
+
+    def drive_teams_on_mesh(local_array):
+        k_all = lax.axis_size("lev")
+        t_next = local_array
+        for src_i in [
+            [(nth, nth ^ no) for nth in range(k_all)] for no in (1, 2, 4, 8, 16) if no < k_all
+        ]:
+            kept_arr = lax.ppermute(t_next, "lev", src_i)
+            t_next = t_next + kept_arr
+        return t_next
+
     nfields, lev_dev, lat_band, lon_count = atmos_fields.shape
     wave_count = wave_order.shape[0]
     table, points = fourier_table(wave_order, lon_count)
@@ -84,7 +95,7 @@
         "ql,qljk->qjk", column_weight, masked, preferred_element_type=jnp.float32
     )
     quarter = lon_count // lax.axis_size("lev")
-    totals = lax.psum(partial_sum, "lev")
+    totals = drive_teams_on_mesh(partial_sum)
     own_flux = lax.dynamic_slice_in_dim(totals, lax.axis_index("lev") * quarter, quarter, 2)
     block_rows = (
         own_flux.reshape(FIELDS, lat_band, quarter // BLOCK, BLOCK)

time: 200 us -> 228 us (1.14)
  waiting for transfers between devices: 75.1 us -> 89 us
  starting transfers between devices: 39.7 us -> 50.6 us
  other arithmetic: 37.9 us -> 40.6 us
    ppermute x0 -> x2, waiting for transfers between devices: none -> 22 us  [drive_teams_on_mesh(): kept_arr = lax.ppermute(t_next, 'lev', src_i)]
    psum x1 -> x0, waiting for transfers between devices: 10.6 us -> none  [body(): totals = lax.psum(partial_sum, 'lev')]
    all_gather x1, waiting for transfers between devices: 14.7 us -> 24.9 us  [body(): lax.all_gather(regrouped, 'lev', axis=1, tiled=True)]
    ppermute x3, waiting for transfers between devices: 11.1 us -> 4.6 us  [with_halo(): lax.ppermute(head, axis, [((i + 1) % count, i) for i in range(ends)])]
    ppermute x0 -> x2, starting transfers between devices: none -> 6.33 us  [drive_teams_on_mesh(): kept_arr = lax.ppermute(t_next, 'lev', src_i)]
    ppermute x3, starting transfers between devices: 20.5 us -> 24.6 us  [with_halo(): lax.ppermute(head, axis, [((i + 1) % count, i) for i in range(ends)])]
    add x0 -> x2, other arithmetic: none -> 2.77 us  [drive_teams_on_mesh(): t_next = t_next + kept_arr]
    ppermute x3, waiting for transfers between devices: 13 us -> 10.5 us  [with_halo(): lax.ppermute(tail, axis, [(i, (i + 1) % count) for i in range(ends)])]
  transfers between devices with their start and end apart: 10 -> 11, of which waited for: 7 -> 7; matrix products, arithmetic and copies ran while one was open for 26% -> 25% of each run, Pallas kernels for 0% -> 0%
where the time goes in v1:
time: 228 us
  waiting for transfers between devices  89 us (39%)
  starting transfers between devices  50.6 us (22%)
  other arithmetic  40.6 us (18%)
  local copies, waits for them, and re-layouts  18.8 us (8%)
  between operations  14.5 us (6%)
  matrix products  14.2 us (6%)
    psum x1, waiting for transfers between devices, body(): tile_sums = lax.psum(arrived, 'lev')  27.1 us
    another operation x1, other arithmetic  25 us
    all_gather x1, waiting for transfers between devices, body(): lax.all_gather(regrouped, 'lev', axis=1, tiled=True)  24.9 us
    ppermute x3, starting transfers between devices, with_halo(): lax.ppermute(head, axis, [((i + 1) % count, i) for i in range(ends)])  24.6 us
    ppermute x2, waiting for transfers between devices, drive_teams_on_mesh(): kept_arr = lax.ppermute(t_next, 'lev', src_i)  22 us
    all_to_all x1, starting transfers between devices, body(): lax.all_to_all(coeffs.transpose(4, 1, 0, 3, 2).reshape(wave_count, lev_de...  13.5 us
    ppermute x3, waiting for transfers between devices, with_halo(): lax.ppermute(tail, axis, [(i, (i + 1) % count) for i in range(ends)])  10.5 us
    ppermute x2, starting transfers between devices, drive_teams_on_mesh(): kept_arr = lax.ppermute(t_next, 'lev', src_i)  6.33 us
  transfers between devices with their start and end apart: 11, of which 7 were waited for; matrix products, arithmetic and copies ran while one was open for 25% of the time, Pallas kernels for 0%

profile of v1, /device:TPU:1, one launch (start us, length us, event | category | flops | bytes accessed | tf_op | source)
XLA Modules:
  0.0 227.7 jit_solution(10624882624344308134)
XLA Ops:
  7.2 0.9 iota_compare_fusion
  8.0 3.6 %broadcast_select_fusion = bf16[2,6,40,5632]{3,2,1,0:T(8,128)(2,1)S(1)} fusion(bf16[2,6,40,5632]{3,2,1,0:T(8,128)(2,1)} %param.9, pred[40,5632]{1,0:T(8,128)(4,1)S(1)} %iota_compare_fusion), kind=kLoop, calls=%fused_computation.16 | loop fusion | flops 2703360 | bytes 11038720 | tf_op jit(solution)/shard_map/jit(_where)/select_n | solution.py:65
  11.7 2.4 %fusion = f32[2,1,40,5632]{3,1,2,0:T(1,128)S(1)} fusion(bf16[2,6,40,5632]{3,2,1,0:T(8,128)(2,1)S(1)} %broadcast_select_fusion, bf16[2,6,1,1]{1,0,2,3:T(2,128)(2,1)S(1)} %bitcast.61), kind=kOutput, calls=%fused_computation.3 | convolution fusion | flops 5406720 | bytes 7208984 | tf_op jit(solution)/shard_map/ql,qljk->qjk/dot_general | solution.py:94
  14.1 1.3 copy.61
  15.5 2.0 collective-permute-start.2
  17.6 25.0 %cosine_convert_fusion = (bf16[5632,256]{0,1:T(8,128)(2,1)S(1)}, bf16[5632,256]{0,1:T(8,128)(2,1)S(1)}) fusion(s32[256]{0:T(256)S(1)} %copy-done.7), kind=kLoop, calls=%fused_computation.9 | loop fusion | flops 17301504 | bytes 5768192 | tf_op jit(solution)/shard_map/convert
  42.6 2.9 %pad_maximum_fusion = bf16[5632,512]{0,1:T(8,128)(2,1)} fusion(bf16[5632,256]{0,1:T(8,128)(2,1)S(1)} %get-tuple-element.21, bf16[5632,256]{0,1:T(8,128)(2,1)S(1)} %get-tuple-element.20), kind=kLoop, calls=%fused_computation.7 | loop fusion | flops 11534336 | bytes 11534336 | tf_op jit(solution)/shard_map/concatenate | solution.py:35
  45.5 10.1 %collective-permute-done.2 = f32[2,40,5632]{2,1,0:T(8,128)} collective-permute-done((f32[2,40,5632]{2,1,0:T(8,128)}, f32[2,40,5632]{2,1,0:T(8,128)}, u32[]{:S(2)}, u32[]{:S(2)}) %collective-permute-start.2) | collective-permute-done | bytes 1802272 | tf_op jit(solution)/shard_map/ppermute | solution.py:57
  55.5 1.7 fusion.42
  57.2 4.3 %collective-permute-start.3 = (f32[2,40,5632]{2,1,0:T(8,128)S(1)}, f32[2,40,5632]{2,1,0:T(8,128)}, u32[]{:S(2)}, u32[]{:S(2)}) collective-permute-start(f32[2,40,5632]{2,1,0:T(8,128)S(1)} %fusion.42), channel_id=1, source_target_pairs={{0,8},{4,12},{8,0},{12,4},{1,9},{5,13},{9,1},{13,5},{2,10},{6,14},... | collective-permute-start | bytes 5406728 | tf_op jit(solution)/shard_map/ppermute | solution.py:57
  61.5 5.7 %fusion.15 = bf16[256,6,2,2,40]{0,4,3,1,2:T(8,128)(2,1)S(1)} fusion(bf16[2,256,5632,1,1]{2,1,0,4,3:T(8,128)(2,1)} %bitcast.63, bf16[2,6,40,5632]{3,2,1,0:T(8,128)(2,1)S(1)} %broadcast_select_fusion, f32[256,40]{0,1:T(8,128)S(1)} %compare_select_fusion), kind=kOutput, calls=%fused_computation.20 | convolution fusion | flops 2768732160 | bytes 11706368 | tf_op jit(solution)/shard_map/dot_general | solution.py:73
  67.2 0.8 copy.31
  68.0 1.8 copy.32
  69.8 3.4 %reshape.235 = bf16[64,2,1920]{2,1,0:T(2,128)(2,1)} reshape(bf16[256,24,40]{2,1,0:T(8,128)(2,1)S(1)} %copy.32) | data formatting | bytes 983040
  73.2 13.5 %all-to-all-start = ((bf16[64,2,1920]{2,1,0:T(2,128)(2,1)}), bf16[64,2,1920]{2,1,0:T(2,128)(2,1)S(1)}, u32[]{:S(2)}, u32[]{:S(2)}) async-start(bf16[64,2,1920]{2,1,0:T(2,128)(2,1)} %reshape.235), calls=%async_computation | async-start | bytes 983040 | tf_op jit(solution)/shard_map/all_to_all | solution.py:76
  86.9 0.1 rem.47
  87.1 0.1 div.26
  87.3 0.1 copy.34
  87.4 0.1 ne.88
  87.5 11.9 %collective-permute-done.3 = f32[2,40,5632]{2,1,0:T(8,128)} collective-permute-done((f32[2,40,5632]{2,1,0:T(8,128)S(1)}, f32[2,40,5632]{2,1,0:T(8,128)}, u32[]{:S(2)}, u32[]{:S(2)}) %collective-permute-start.3) | collective-permute-done | bytes 1802272 | tf_op jit(solution)/shard_map/ppermute | solution.py:57
  99.4 1.1 dynamic-slice_add_fusion
  100.6 0.3 copy.37
  101.0 3.1 %scatter_custom_fusion = f32[816,256]{1,0:T(8,128)S(1)} fusion(s32[440]{0:T(512)S(1)} %bitcast.80, f32[55,8,2,128]{3,2,1,0:T(2,128)S(1)} %bitcast.74, f32[]{:T(128)} %constant.40.clone.1), kind=kCustom, calls=%fused_computation.35 | custom fusion | flops 112640 | bytes 1286148 | tf_op jit(solution)/shard_map/scatter-add | solution.py:105
  104.2 10.5 %collective-permute-start.5 = (f32[272,256]{1,0:T(8,128)S(1)}, f32[272,256]{1,0:T(8,128)S(1)}, u32[]{:S(2)}, u32[]{:S(2)}) collective-permute-start(f32[272,256]{1,0:T(8,128)S(1)} %get-tuple-element.9), channel_id=1, source_target_pairs={{1,0},{2,1},{3,2},{16,3},{17,16},{18,17},{19,18},{32,19},{33,32},{... | collective-permute-start | bytes 835592 | tf_op jit(solution)/shard_map/ppermute | solution.py:24
  114.7 2.1 collective-permute-start.4
  116.7 4.3 %collective-permute-done.5 = f32[272,256]{1,0:T(8,128)S(1)} collective-permute-done((f32[272,256]{1,0:T(8,128)S(1)}, f32[272,256]{1,0:T(8,128)S(1)}, u32[]{:S(2)}, u32[]{:S(2)}) %collective-permute-start.5) | collective-permute-done | bytes 278560 | tf_op jit(solution)/shard_map/ppermute | solution.py:24
  121.0 10.5 %collective-permute-done.4 = f32[272,256]{1,0:T(8,128)S(1)} collective-permute-done((f32[272,256]{1,0:T(8,128)S(1)}, f32[272,256]{1,0:T(8,128)S(1)}, u32[]{:S(2)}, u32[]{:S(2)}) %collective-permute-start.4) | collective-permute-done | bytes 278560 | tf_op jit(solution)/shard_map/ppermute | solution.py:22
  131.5 0.1 reshape.210
  131.7 0.8 reshape.211
  132.5 0.3 all-gather.2.cloned.1.call-start
  132.8 2.5 %reshape.236 = bf16[256,24,40]{2,1,0:T(8,128)(2,1)S(1)} reshape(bf16[64,2,1920]{2,1,0:T(2,128)(2,1)S(1)} %all-to-all-done) | data formatting | bytes 983040
  135.3 0.6 copy.33
  135.9 3.9 %all_to_all.16 = bf16[4,24,2560]{2,1,0:T(8,128)(2,1)} reshape(bf16[4,24,64,40]{3,2,1,0:T(8,128)(2,1)S(1)} %copy.33) | data formatting | bytes 983040 | tf_op jit(solution)/shard_map/all_to_all | solution.py:76
  139.8 1.9 collective-permute-start.1
  141.8 5.8 %collective-permute-start = (f32[2,1,2176]{2,1,0:T(1,128)S(1)}, f32[2,1,2176]{2,1,0:T(1,128)S(1)}, u32[]{:S(2)}, u32[]{:S(2)}) collective-permute-start(f32[2,1,2176]{2,1,0:T(1,128)S(1)} %get-tuple-element.16), channel_id=1, source_target_pairs={{1,0},{2,1},{3,2},{16,3},{17,16},{18,17},{19,18},{32,19},{33,32},{... | collective-permute-start | bytes 52232 | tf_op jit(solution)/shard_map/ppermute | solution.py:24
  147.6 0.1 fusion.23
  147.9 0.1 copy.39
  148.0 0.3 collective-permute-done
  148.4 27.1 %all-reduce.2.cloned.1.call-done = f32[2,16,2176]{2,1,0:T(8,128)} async-done(((f32[2,16,2176]{2,1,0:T(8,128)}), f32[2,16,2176]{2,1,0:T(8,128)}) %all-reduce.2.cloned.1.call-update) | async-done | bytes 278544 | tf_op jit(solution)/shard_map/psum | solution.py:110
  175.5 1.2 fusion.31
  176.7 0.7 slice_bitcast_fusion
  177.3 8.4 %collective-permute-start.7 = (f32[16,2176]{1,0:T(8,128)S(1)}, f32[16,2176]{1,0:T(8,128)S(1)}, u32[]{:S(2)}, u32[]{:S(2)}) collective-permute-start(f32[16,2176]{1,0:T(8,128)S(1)} %get-tuple-element.11), channel_id=1, source_target_pairs={{1,0},{2,1},{3,2},{16,3},{17,16},{18,17},{19,18},{32,19},{33,32},{... | collective-permute-start | bytes 417800 | tf_op jit(solution)/shard_map/ppermute | solution.py:24
  185.8 1.9 collective-permute-start.6
  187.7 24.9 %all-gather.2.cloned.1.call-done = bf16[4,96,2560]{2,1,0:T(8,128)(2,1)} async-done(((bf16[4,24,2560]{2,1,0:T(8,128)(2,1)}), bf16[4,96,2560]{2,1,0:T(8,128)(2,1)}) %all-gather.2.cloned.1.call-update) | async-done | bytes 1966096 | tf_op jit(solution)/shard_map/all_gather | solution.py:85
  212.6 6.1 %fusion.45 = f32[4,96,384]{2,1,0:T(8,128)} fusion(bf16[4,96,2560]{2,1,0:T(8,128)(2,1)} %all-gather.2.cloned.1.call-done, bf16[4,2560,384]{2,1,0:T(8,128)(2,1)} %param.12), kind=kOutput, calls=%fused_computation.88 | convolution fusion | flops 754974720 | bytes 10420224 | tf_op jit(solution)/shard_map/srj,sjd->srd/dot_general | solution.py:83
  218.7 1.2 gather_fusion
  219.9 0.1 broadcast_in_dim.68
  220.1 0.8 select_select_fusion
  (45 shorter events, 1.0 us)
Async XLA Ops:
  7.2 4.5 %copy-start = (bf16[2,6]{1,0:T(2,128)(2,1)S(1)}, bf16[2,6]{1,0:T(2,128)(2,1)}, u32[]{:S(2)}) copy-start(bf16[2,6]{1,0:T(2,128)(2,1)} %param.13) | copy-start | bytes 76
  11.7 5.8 %copy-start.6 = (s32[40]{0:T(128)S(1)}, s32[40]{0:T(128)}, u32[]{:S(2)}) copy-start(s32[40]{0:T(128)} %param.10) | copy-start | bytes 484
  11.7 5.8 %copy-start.7 = (s32[256]{0:T(256)S(1)}, s32[256]{0:T(256)}, u32[]{:S(2)}) copy-start(s32[256]{0:T(256)} %param.11) | copy-start | bytes 3076
  15.5 40.0 %collective-permute-start.2 = (f32[2,40,5632]{2,1,0:T(8,128)}, f32[2,40,5632]{2,1,0:T(8,128)}, u32[]{:S(2)}, u32[]{:S(2)}) collective-permute-start(f32[2,40,5632]{2,1,0:T(8,128)} %bitcast.59), channel_id=1, source_target_pairs={{0,4},{4,0},{8,12},{12,8},{1,5},{5,1},{9,13},{13,9},{2,6},{6,2},{1... | collective-permute-start | bytes 5406728 | tf_op jit(solution)/shard_map/ppermute | solution.py:57
  57.2 42.2 %collective-permute-start.3 = (f32[2,40,5632]{2,1,0:T(8,128)S(1)}, f32[2,40,5632]{2,1,0:T(8,128)}, u32[]{:S(2)}, u32[]{:S(2)}) collective-permute-start(f32[2,40,5632]{2,1,0:T(8,128)S(1)} %fusion.42), channel_id=1, source_target_pairs={{0,8},{4,12},{8,0},{12,4},{1,9},{5,13},{9,1},{13,5},{2,10},{6,14},... | collective-permute-start | bytes 5406728 | tf_op jit(solution)/shard_map/ppermute | solution.py:57
  67.2 19.6 %copy-start.4 = (s32[40,11]{0,1:T(8,128)S(1)}, s32[40,11]{0,1:T(8,128)}, u32[]{:S(2)}) copy-start(s32[40,11]{0,1:T(8,128)} %param.14) | copy-start | bytes 5284
  73.2 59.5 %all-to-all-start = ((bf16[64,2,1920]{2,1,0:T(2,128)(2,1)}), bf16[64,2,1920]{2,1,0:T(2,128)(2,1)S(1)}, u32[]{:S(2)}, u32[]{:S(2)}) async-start(bf16[64,2,1920]{2,1,0:T(2,128)(2,1)} %reshape.235), calls=%async_computation | async-start | bytes 983040 | tf_op jit(solution)/shard_map/all_to_all | solution.py:76
  86.7 88.8 %all-reduce.2.cloned.1.call-start = ((), (), s32[]{:S(2)}) async-start(), calls=%async_computation.2 | async-start | bytes 557056 | tf_op jit(solution)/shard_map/psum | solution.py:110
  104.2 16.8 %collective-permute-start.5 = (f32[272,256]{1,0:T(8,128)S(1)}, f32[272,256]{1,0:T(8,128)S(1)}, u32[]{:S(2)}, u32[]{:S(2)}) collective-permute-start(f32[272,256]{1,0:T(8,128)S(1)} %get-tuple-element.9), channel_id=1, source_target_pairs={{1,0},{2,1},{3,2},{16,3},{17,16},{18,17},{19,18},{32,19},{33,32},{... | collective-permute-start | bytes 835592 | tf_op jit(solution)/shard_map/ppermute | solution.py:24
  114.6 25.2 %copy-start.1 = (f32[16,2176]{1,0:T(8,128)S(1)}, f32[16,2176]{1,0:T(8,128)}, u32[]{:S(2)}) copy-start(f32[16,2176]{1,0:T(8,128)} %param.15) | copy-start | bytes 417796
  114.6 25.2 %copy-start.2 = (f32[16,2176]{1,0:T(8,128)S(1)}, f32[16,2176]{1,0:T(8,128)}, u32[]{:S(2)}) copy-start(f32[16,2176]{1,0:T(8,128)} %param.16) | copy-start | bytes 417796
  114.7 16.8 %collective-permute-start.4 = (f32[272,256]{1,0:T(8,128)S(1)}, f32[272,256]{1,0:T(8,128)S(1)}, u32[]{:S(2)}, u32[]{:S(2)}) collective-permute-start(f32[272,256]{1,0:T(8,128)S(1)} %get-tuple-element.8), channel_id=1, source_target_pairs={{0,1},{1,2},{2,3},{3,16},{16,17},{17,18},{18,19},{19,32},{32,33},{... | collective-permute-start | bytes 835592 | tf_op jit(solution)/shard_map/ppermute | solution.py:22
  131.5 16.1 %copy-start.5 = (s32[16,17]{1,0:T(8,128)S(1)}, s32[16,17]{1,0:T(8,128)}, u32[]{:S(2)}) copy-start(s32[16,17]{1,0:T(8,128)} %param.17) | copy-start | bytes 3268
  132.5 80.1 %all-gather.2.cloned.1.call-start = ((), (), s32[]{:S(2)}) async-start(), calls=%async_computation.1 | async-start | bytes 2457600 | tf_op jit(solution)/shard_map/all_gather | solution.py:85
  139.8 8.2 %collective-permute-start.1 = (f32[2,1,2176]{2,1,0:T(1,128)S(1)}, f32[2,1,2176]{2,1,0:T(1,128)S(1)}, u32[]{:S(2)}, u32[]{:S(2)}) collective-permute-start(f32[2,1,2176]{2,1,0:T(1,128)S(1)} %get-tuple-element.17), channel_id=1, source_target_pairs={{0,1},{1,2},{2,3},{3,16},{16,17},{17,18},{18,19},{19,32},{32,33},{... | collective-permute-start | bytes 52232 | tf_op jit(solution)/shard_map/ppermute | solution.py:22
  141.8 6.6 %collective-permute-start = (f32[2,1,2176]{2,1,0:T(1,128)S(1)}, f32[2,1,2176]{2,1,0:T(1,128)S(1)}, u32[]{:S(2)}, u32[]{:S(2)}) collective-permute-start(f32[2,1,2176]{2,1,0:T(1,128)S(1)} %get-tuple-element.16), channel_id=1, source_target_pairs={{1,0},{2,1},{3,2},{16,3},{17,16},{18,17},{19,18},{32,19},{33,32},{... | collective-permute-start | bytes 52232 | tf_op jit(solution)/shard_map/ppermute | solution.py:24
  177.3 41.3 %copy-start.3 = (f32[16,2176]{1,0:T(8,128)}, f32[16,2176]{1,0:T(8,128)S(1)}, u32[]{:S(2)}) copy-start(f32[16,2176]{1,0:T(8,128)S(1)} %get-tuple-element.11) | copy-start | bytes 417796
  177.3 41.3 %collective-permute-start.7 = (f32[16,2176]{1,0:T(8,128)S(1)}, f32[16,2176]{1,0:T(8,128)S(1)}, u32[]{:S(2)}, u32[]{:S(2)}) collective-permute-start(f32[16,2176]{1,0:T(8,128)S(1)} %get-tuple-element.11), channel_id=1, source_target_pairs={{1,0},{2,1},{3,2},{16,3},{17,16},{18,17},{19,18},{32,19},{33,32},{... | collective-permute-start | bytes 417800 | tf_op jit(solution)/shard_map/ppermute | solution.py:24
  185.8 32.8 %collective-permute-start.6 = (f32[16,2176]{1,0:T(8,128)S(1)}, f32[16,2176]{1,0:T(8,128)S(1)}, u32[]{:S(2)}, u32[]{:S(2)}) collective-permute-start(f32[16,2176]{1,0:T(8,128)S(1)} %get-tuple-element.11), channel_id=1, source_target_pairs={{0,1},{1,2},{2,3},{3,16},{16,17},{17,18},{18,19},{19,32},{32,33},{... | collective-permute-start | bytes 417800 | tf_op jit(solution)/shard_map/ppermute | solution.py:22
Sparse Core Ops, SparseCore 0:
  132.6 42.8 all-reduce.1
  177.9 34.6 all-gather.1
